TPU v7x, 128 devices: a whole 4x4x4 slice. The times are simulated.
128 devices in a mesh: basis: 64 (over y_hi, z, x, core), grp: 2 (over y_lo).
Axes of the slice: x: 4, y: 4 (y_hi: 2, y_lo: 2; y = y_hi * 2 + y_lo), z: 4, core: 2. Of those that a mesh axis runs over, the one named last changes fastest.
Arguments:
- bra: bfloat16 [262144, 4096], P('basis', 'grp'), may hold values from -0.01171875 to 0.01171875
- dipole: bfloat16 [2048, 8, 128, 128], P('basis'), may hold values from -6 to 6
- block_cols: int32 [2048, 8], P('basis'), may hold values from 0 to 2047, as said below
- ket: bfloat16 [262144, 512], P('basis', 'grp'), may hold values from -0.1875 to 0.1875
- j_upper: int32 [4096], P('grp'), may hold values from 0 to 6
- sym_upper: int32 [4096], P('grp'), may hold values from 0 to 1
- j_lower: int32 [512], replicated, may hold values from 0 to 6
- sym_lower: int32 [512], replicated, may hold values from 0 to 1
Outputs:
- strength: float32 [512, 4096], P('basis', 'grp')
Inputs may be any that keep to these rules, and one draw needn't show every extreme that they name: block_cols[r, 0] = r, and every entry lies within 8 of its row r; entries of one row differ except where clipped to the range's ends.
All inputs are finite; a program needn't handle non-finite values.
Results may differ from a plain program's by a relative error of at most 0.0033.
Values may be sent and summed in bfloat16 or wider, within the bound.
A program may use at most 128 MiB of HBM per device.

v0:
```python
import jax
import jax.numpy as jnp
from jax import lax
from jax.sharding import PartitionSpec as P

REACH = 8


def with_halo(cells, sides, width):
    for axis, dim in sides:
        count = lax.axis_size(axis)
        ends = count - 1
        head = lax.slice_in_dim(cells, 0, width, axis=dim)
        tail = lax.slice_in_dim(cells, cells.shape[dim] - width, cells.shape[dim], axis=dim)
        cells = jnp.concatenate(
            [
                lax.ppermute(tail, axis, [(i, (i + 1) % count) for i in range(ends)]),
                cells,
                lax.ppermute(head, axis, [((i + 1) % count, i) for i in range(ends)]),
            ],
            axis=dim,
        )
    return cells


def from_behind(block, axis, distance):
    devices = range(lax.axis_size(axis))
    route = [((i - distance) % len(devices), i) for i in devices]
    return lax.ppermute(block, axis, route)


def apply_dipole(panel, dipole, block_cols, me_basis):
    rows = panel.shape[0]
    width = panel.shape[1]
    blk = dipole.shape[2]
    nbr = rows // blk
    extended = with_halo(panel, (("basis", 0),), REACH * blk)
    ext_blocks = extended.reshape(nbr + 2 * REACH, blk, width)
    local_cols = block_cols - (me_basis * nbr - REACH)
    picked = ext_blocks[local_cols]
    applied = jnp.einsum("rkij,rkjp->rip", dipole, picked, preferred_element_type=jnp.float32)
    return applied.reshape(rows, width).astype(jnp.bfloat16)


def contract(applied, bra):
    return lax.dot_general(
        applied, bra, (((0,), (0,)), ((), ())), preferred_element_type=jnp.float32
    )


def on_device(bra, dipole, block_cols, ket, j_upper, sym_upper, j_lower, sym_lower):
    me_basis = lax.axis_index("basis")
    me_group = lax.axis_index("grp")
    other_ket = from_behind(ket, "grp", 1)
    own_applied = apply_dipole(ket, dipole, block_cols, me_basis)
    other_applied = apply_dipole(other_ket, dipole, block_cols, me_basis)
    own_moment = contract(own_applied, bra)
    other_moment = contract(other_applied, bra)
    partial_value = jnp.where(
        me_group == 0,
        jnp.concatenate([own_moment, other_moment], axis=0),
        jnp.concatenate([other_moment, own_moment], axis=0),
    )
    lower_rows = partial_value.shape[0] // lax.axis_size("basis")
    total = lax.psum(partial_value, "basis")
    moment = lax.dynamic_slice_in_dim(total, me_basis * lower_rows, lower_rows, 0)
    my_j = lax.dynamic_slice_in_dim(j_lower, me_basis * lower_rows, lower_rows, 0)
    my_sym = lax.dynamic_slice_in_dim(sym_lower, me_basis * lower_rows, lower_rows, 0)
    allowed = (jnp.abs(my_j[:, None] - j_upper[None, :]) <= 1) & (
        my_sym[:, None] != sym_upper[None, :]
    )
    return jnp.where(allowed, moment * moment, jnp.zeros_like(moment))


def solution(mesh):
    return jax.shard_map(
        on_device,
        mesh=mesh,
        in_specs=(
            P("basis", "grp"),
            P("basis", None, None, None),
            P("basis", None),
            P("basis", "grp"),
            P("grp"),
            P("grp"),
            P(),
            P(),
        ),
        out_specs=P("basis", "grp"),
        check_vma=False,
    )
```

profile of v0, /device:TPU:8, one launch (start us, length us, event | category | flops | bytes accessed | tf_op | source)
XLA Modules:
  0.0 771.5 jit_solution(9998369961491888677)
XLA Ops:
  6.5 0.0 all-reduce.2.cloned.1.call-start
  6.5 1.3 fusion.1
  7.8 1.8 collective-permute-start
  9.6 1.3 collective-permute-start.1
  10.9 0.1 collective-permute-start.2
  11.0 0.7 compare_select_fusion
  11.7 0.1 copy.9
  11.8 0.1 reshape.18
  11.9 0.0 collective-permute-done
  11.9 0.0 copy-start.1
  11.9 0.8 copy-done.1
  12.7 2.1 collective-permute-done.1
  14.8 2.1 pad_maximum_fusion
  16.9 9.8 %gather_fusion = bf16[256,128,256]{2,1,0:T(8,128)(2,1)} fusion(bf16[48,128,256]{2,1,0:T(8,128)(2,1)S(1)} %bitcast.25, s32[1024]{0:T(1024)S(1)} %pad_clamp_fusion), kind=kCustom, calls=%fused_computation | custom fusion | bytes 33555456 | tf_op jit(solution)/shard_map/gather | solution.py:40
  26.6 11.1 %bitcast_convert_fusion.1 = bf16[32,256,128]{1,2,0:T(8,128)(2,1)S(1)} fusion(bf16[32,8,128,128]{3,2,1,0:T(8,128)(2,1)} %param.9, bf16[32,8,128,256]{3,2,1,0:T(8,128)(2,1)} %bitcast.27), kind=kOutput, calls=%fused_computation.4 | convolution fusion | flops 2148532224 | bytes 27262976 | tf_op jit(solution)/shard_map/rkij,rkjp->rip/dot_general | solution.py:41
  37.7 20.6 %collective-permute-done.2 = bf16[4096,256]{1,0:T(8,128)(2,1)} collective-permute-done((bf16[4096,256]{1,0:T(8,128)(2,1)}, bf16[4096,256]{1,0:T(8,128)(2,1)}, u32[]{:S(2)}, u32[]{:S(2)}) %collective-permute-start.2) | collective-permute-done | bytes 2097184 | tf_op jit(solution)/shard_map/ppermute | solution.py:29
  58.3 1.3 fusion.2
  59.6 3.2 collective-permute-start.3
  62.8 1.5 collective-permute-start.4
  64.3 9.5 %fusion.3 = f32[256,2048]{1,0:T(8,128)} fusion(bf16[4096,256]{1,0:T(8,128)(2,1)S(1)} %bitcast.28, bf16[4096,2048]{1,0:T(8,128)(2,1)} %param.8), kind=kOutput, calls=%fused_computation.14 | convolution fusion | flops 4294967296 | bytes 20971520 | tf_op jit(solution)/shard_map/dot_general | solution.py:46
  73.8 0.0 collective-permute-done.3
  73.8 0.0 collective-permute-done.4
  73.8 1.8 pad_maximum_fusion.1
  75.7 9.8 %gather_fusion.1 = bf16[256,128,256]{2,1,0:T(8,128)(2,1)} fusion(bf16[48,128,256]{2,1,0:T(8,128)(2,1)S(1)} %bitcast.24, s32[1024]{0:T(1024)S(1)} %pad_clamp_fusion), kind=kCustom, calls=%fused_computation.1 | custom fusion | bytes 33555456 | tf_op jit(solution)/shard_map/gather | solution.py:40
  85.4 11.1 %bitcast_convert_fusion = bf16[32,256,128]{1,2,0:T(8,128)(2,1)S(1)} fusion(bf16[32,8,128,128]{3,2,1,0:T(8,128)(2,1)} %param.9, bf16[32,8,128,256]{3,2,1,0:T(8,128)(2,1)} %bitcast.26), kind=kOutput, calls=%fused_computation.3 | convolution fusion | flops 2148532224 | bytes 27262976 | tf_op jit(solution)/shard_map/rkij,rkjp->rip/dot_general | solution.py:41
  96.5 0.0 copy-start
  96.5 8.3 %fusion.4 = f32[256,2048]{1,0:T(8,128)S(1)} fusion(bf16[4096,256]{1,0:T(8,128)(2,1)S(1)} %bitcast.29, bf16[4096,2048]{1,0:T(8,128)(2,1)} %param.8), kind=kOutput, calls=%fused_computation.15 | convolution fusion | flops 4294967296 | bytes 20971520 | tf_op jit(solution)/shard_map/dot_general | solution.py:46
  104.8 0.0 copy-done
  104.9 2.3 maximum_select_fusion
  107.2 0.0 copy-start.2
  107.2 0.0 copy-start.3
  107.2 0.0 all-reduce.2.cloned.1.call-update
  107.2 0.8 dynamic_slice.10
  108.0 0.8 dynamic_slice.9
  108.7 654.4 %all-reduce.2.cloned.1.call-done = f32[512,2048]{1,0:T(8,128)} async-done(((f32[512,2048]{1,0:T(8,128)}), f32[512,2048]{1,0:T(8,128)}) %all-reduce.2.cloned.1.call-update) | async-done | bytes 4194320 | tf_op jit(solution)/shard_map/psum | solution.py:65
  763.1 0.0 copy-done.2
  763.1 0.0 copy-done.3
  763.1 1.6 multiply_select_fusion
  (1 shorter events, 0.0 us)
Async XLA Ops:
  6.5 756.6 %all-reduce.2.cloned.1.call-start = ((), (), s32[]{:S(2)}) async-start(), calls=%async_computation | async-start | bytes 8388608 | tf_op jit(solution)/shard_map/psum | solution.py:65
  7.8 4.1 collective-permute-start
  9.6 5.2 collective-permute-start.1
  10.9 47.4 %collective-permute-start.2 = (bf16[4096,256]{1,0:T(8,128)(2,1)}, bf16[4096,256]{1,0:T(8,128)(2,1)}, u32[]{:S(2)}, u32[]{:S(2)}) collective-permute-start(bf16[4096,256]{1,0:T(8,128)(2,1)} %param.11), channel_id=1, source_target_pairs={{1,0},{0,1},{3,2},{2,3},{5,4},{4,5},{7,6},{6,7},{9,8},{8,9},{11,10... | collective-permute-start | bytes 6291464 | tf_op jit(solution)/shard_map/ppermute | solution.py:29
  11.9 0.8 copy-start.1
  59.6 14.2 %collective-permute-start.3 = (bf16[1024,256]{1,0:T(8,128)(2,1)S(1)}, bf16[1024,256]{1,0:T(8,128)(2,1)S(1)}, u32[]{:S(2)}, u32[]{:S(2)}) collective-permute-start(bf16[1024,256]{1,0:T(8,128)(2,1)S(1)} %get-tuple-element.7), channel_id=1, source_target_pairs={{0,2},{2,4},{4,6},{6,8},{8,10},{10,12},{12,14},{14,16},{16,18},{18... | collective-permute-start | bytes 1572872 | tf_op jit(solution)/shard_map/ppermute | solution.py:17
  62.8 11.0 %collective-permute-start.4 = (bf16[1024,256]{1,0:T(8,128)(2,1)S(1)}, bf16[1024,256]{1,0:T(8,128)(2,1)S(1)}, u32[]{:S(2)}, u32[]{:S(2)}) collective-permute-start(bf16[1024,256]{1,0:T(8,128)(2,1)S(1)} %get-tuple-element.8), channel_id=1, source_target_pairs={{2,0},{4,2},{6,4},{8,6},{10,8},{12,10},{14,12},{16,14},{18,16},{20... | collective-permute-start | bytes 1572872 | tf_op jit(solution)/shard_map/ppermute | solution.py:19
  96.5 8.3 %copy-start = (f32[256,2048]{1,0:T(8,128)S(1)}, f32[256,2048]{1,0:T(8,128)}, u32[]{:S(2)}) copy-start(f32[256,2048]{1,0:T(8,128)} %fusion.3) | copy-start | bytes 6291460
  107.2 655.9 %copy-start.2 = (s32[2048]{0:T(1024)S(1)}, s32[2048]{0:T(1024)}, u32[]{:S(2)}) copy-start(s32[2048]{0:T(1024)} %param.13) | copy-start | bytes 24580
  107.2 655.9 %copy-start.3 = (s32[2048]{0:T(1024)S(1)}, s32[2048]{0:T(1024)}, u32[]{:S(2)}) copy-start(s32[2048]{0:T(1024)} %param.12) | copy-start | bytes 24580
Sparse Core Ops, SparseCore 0:
  107.3 655.7 all-reduce.1
where the time goes:
time: 773 us; the launch traced here: 771 us
  waiting for transfers between devices  677 us (88%)
  matrix products  40 us (5%)
  local copies, waits for them, and re-layouts  24.5 us (3%)
  between operations  13.5 us (2%)
  other arithmetic  8.51 us (1%)
  starting transfers between devices  7.84 us (1%)
    psum x1, waiting for transfers between devices, on_device(): total = lax.psum(partial_value, 'basis')  654 us
    dot_general x2, matrix products, apply_dipole(): jnp.einsum('rkij,rkjp->rip', dipole, picked, preferred_element_type=jnp.f...  22.2 us
    ppermute x1, waiting for transfers between devices, from_behind(): return lax.ppermute(block, axis, route)  20.6 us
    gather x2, local copies, waits for them, and re-layouts, apply_dipole(): picked = ext_blocks[local_cols]  19.5 us
    dot_general x2, matrix products, contract(): lax.dot_general(applied, bra, (((0,), (0,)), ((), ())), preferred_element...  17.8 us
  transfers between devices with their start and end apart: 6, of which 3 were waited for; matrix products, arithmetic and copies ran while one was open for 5% of the time, Pallas kernels for 0%

commit v1 on v0

v1 whole, which is shorter than its diff:
```python
import jax
import jax.numpy as jnp
from jax import lax
from jax.experimental import pallas as pl
from jax.experimental.pallas import tpu as pltpu
from jax.sharding import PartitionSpec as P

MESH = pl.DeviceIdType.MESH
F32 = jnp.float32
BF16 = jnp.bfloat16

REACH = 8
BLK = 128
PLANE = 32
SEG = 16
NT = 256

CHUNKS = ((0, 4), (4, 2), (6, 1), (7, 1))


def pieces_of(chunk):
    if chunk == 0:
        return ((8, 4), (12, 4), (16, 4), (20, 4), (0, 4), (4, 4), (24, 4), (28, 4))
    return ((8, 8), (16, 8), (0, 8), (24, 8))


PIECES = tuple((c, r0, n) for c in range(len(CHUNKS)) for r0, n in pieces_of(c))
DIP_ROWS = 4
DIP_ORDER = (2, 3, 4, 5, 0, 1, 6, 7)


def kernel(
    cols, jl, sl, ju, su, bra_hbm, dip_hbm, ket_hbm, out,
    bra, dip, ket_own, ket_ext, perm, app_own, app_oth, stage,
    sb_own, rb_own, sb0, rb0, sb1, rb1, sb2, rb2, sb3, rb3,
    sum_own, sum_oth, sum_in,
    bra_sem, dip_sem, ket_sem, halo_send, halo_recv, y_send, y_recv, a_send, a_recv, s_send, s_recv,
):
    b = lax.axis_index("basis")
    g = lax.axis_index("grp")
    yh = b // PLANE
    me = b % PLANE
    nbr = dip_hbm.shape[0]
    last = 2 * PLANE - 1
    mine = yh == g

    ket_copies = [
        pltpu.make_async_copy(ket_hbm, ket_own, ket_sem.at[0]),
        pltpu.make_async_copy(ket_hbm, ket_ext.at[pl.ds(REACH, nbr)], ket_sem.at[1]),
    ]
    dip_copies = {}
    for i in DIP_ORDER:
        rows = pl.ds(i * DIP_ROWS, DIP_ROWS)
        dip_copies[i] = pltpu.make_async_copy(dip_hbm.at[rows], dip.at[rows], dip_sem.at[i])
    bra_copies = [
        pltpu.make_async_copy(bra_hbm.at[:, pl.ds(n * NT, NT)], bra.at[n], bra_sem.at[n])
        for n in range(bra.shape[0])
    ]
    ket_copies[0].start()
    for i in DIP_ORDER[:4]:
        dip_copies[i].start()
    ket_copies[1].start()
    for i in DIP_ORDER[4:]:
        dip_copies[i].start()
    for copy in bra_copies:
        copy.start()

    barrier = pltpu.get_barrier_semaphore()

    def greet(s, carry):
        peer = yh * PLANE + lax.rem(me + s, PLANE)
        pl.semaphore_signal(barrier, inc=1, device_id=(peer, g), device_id_type=MESH)
        return carry

    lax.fori_loop(1, PLANE, greet, 0)
    across = ((1 - yh) * PLANE + me, g)
    partner = (b, 1 - g)
    pl.semaphore_signal(barrier, inc=1, device_id=across, device_id_type=MESH)
    pl.semaphore_signal(barrier, inc=1, device_id=partner, device_id_type=MESH)

    @pl.when(b == PLANE - 1)
    def _():
        pl.semaphore_signal(barrier, inc=1, device_id=(PLANE, g), device_id_type=MESH)

    @pl.when(b == PLANE)
    def _():
        pl.semaphore_signal(barrier, inc=1, device_id=(PLANE - 1, g), device_id_type=MESH)

    size = perm.shape[0]
    place = lax.broadcasted_iota(jnp.int32, (size, size), 0)
    state = lax.broadcasted_iota(jnp.int32, (size, size), 1)
    wanted = (place & (PLANE - 1)) * 8 + (place >> 5)
    perm[...] = jnp.where(state == wanted, 1.0, 0.0).astype(BF16)

    pl.semaphore_wait(barrier, PLANE + 1 + jnp.where((b == PLANE - 1) | (b == PLANE), 1, 0))

    to_next = pltpu.make_async_remote_copy(
        ket_hbm.at[pl.ds(nbr - REACH, REACH)], ket_ext.at[pl.ds(0, REACH)],
        halo_send.at[0], halo_recv.at[0], device_id=(jnp.minimum(b + 1, last), g), device_id_type=MESH,
    )
    to_prev = pltpu.make_async_remote_copy(
        ket_hbm.at[pl.ds(0, REACH)], ket_ext.at[pl.ds(REACH + nbr, REACH)],
        halo_send.at[1], halo_recv.at[1], device_id=(jnp.maximum(b - 1, 0), g), device_id_type=MESH,
    )

    @pl.when(b < last)
    def _():
        to_next.start()

    @pl.when(b > 0)
    def _():
        to_prev.start()

    y_copies = []
    for i, (c, r0, n) in enumerate(PIECES):
        e0, ne = CHUNKS[c]
        part = (pl.ds(e0 * PLANE, ne * PLANE), pl.ds(r0 * BLK, n * BLK))
        y_copies.append(
            pltpu.make_async_remote_copy(
                app_own.at[part], app_oth.at[part], y_send.at[i], y_recv.at[i],
                device_id=partner, device_id_type=MESH,
            )
        )

    def apply_rows(r0, n, ket, base):
        def one(i, carry):
            r = r0 + i
            top = ket.shape[0] - 1
            blocks = [ket[jnp.clip(cols[r, k] - base, 0, top)] for k in range(cols.shape[1])]
            row = jnp.concatenate([dip[r, k] for k in range(cols.shape[1])], axis=1)
            value = jnp.dot(row, jnp.concatenate(blocks, axis=0), preferred_element_type=F32)
            turned = lax.dot_general(
                perm[...], value.astype(BF16), (((1,), (1,)), ((), ())), preferred_element_type=F32
            )
            app_own[:, pl.ds(pl.multiple_of(r * BLK, BLK), BLK)] = turned.astype(BF16)
            return carry

        lax.fori_loop(0, n, one, 0)

    ket_copies[0].wait()
    for i, (c, r0, n) in enumerate(PIECES):
        if c > 0:
            y_copies[i].start()
            continue
        dip_copies[r0 // DIP_ROWS].wait()
        if i == 4:
            ket_copies[1].wait()

            @pl.when(b > 0)
            def _():
                to_next.wait_recv()

            @pl.when(b < last)
            def _():
                to_prev.wait_recv()

        if REACH <= r0 and r0 + n <= nbr - REACH:
            apply_rows(r0, n, ket_own, b * nbr)
        else:
            apply_rows(r0, n, ket_ext, b * nbr - REACH)
        y_copies[i].start()

    def contract(lhs, e0, ne, k0, kw, add):
        rows = ne * PLANE

        def one(n, carry):
            value = jnp.dot(
                lhs[pl.ds(e0 * PLANE, rows), pl.ds(k0, kw)], bra[n, pl.ds(k0, kw), :],
                preferred_element_type=F32,
            )
            for h in range(NT // 128):
                for q in range(rows // 8):
                    e, o = q // (PLANE // 8), (q % (PLANE // 8)) * 8
                    at = pl.ds(o * SEG * ne + e * SEG + n * (NT // 128) + h, 8, stride=SEG * ne)
                    tile = value[q * 8:q * 8 + 8, h * 128:h * 128 + 128]
                    if add:
                        tile = stage[at, :] + tile
                    stage[at, :] = tile
            return carry

        lax.fori_loop(0, bra.shape[0], one, 0)

    def scatter(ne, sb, rb, sem):
        rows = ne * SEG

        def cast(o, carry):
            at = pl.ds(pl.multiple_of(o * 4 * rows, 4 * rows), 4 * rows)
            sb[at, :] = stage[at, :].astype(BF16)
            return carry

        lax.fori_loop(0, PLANE // 4, cast, 0)

        def send(s, carry):
            owner = lax.rem(me + s, PLANE)
            pltpu.make_async_remote_copy(
                sb.at[pl.ds(pl.multiple_of(owner * rows, rows), rows)],
                rb.at[pl.ds(pl.multiple_of(s * rows, rows), rows)],
                a_send.at[sem], a_recv.at[sem],
                device_id=(yh * PLANE + owner, g), device_id_type=MESH,
            ).start()
            return carry

        lax.fori_loop(1, PLANE, send, 0)

    def gather(ne, sb, rb, sem, total, e0):
        rows = ne * SEG
        pltpu.make_async_remote_copy(
            sb.at[pl.ds(0, (PLANE - 1) * rows)], rb.at[pl.ds(rows, (PLANE - 1) * rows)],
            a_send.at[sem], a_recv.at[sem], device_id=partner, device_id_type=MESH,
        ).wait()

        def one(s, value):
            return value + rb[pl.ds(pl.multiple_of(s * rows, rows), rows), :].astype(F32)

        value = sb[pl.ds(pl.multiple_of(me * rows, rows), rows), :].astype(F32)
        total[pl.ds(e0 * SEG, rows), :] = lax.fori_loop(1, PLANE, one, value)

    def hop(total, e0, ne, sem):
        part = pl.ds(e0 * SEG, ne * SEG)
        return pltpu.make_async_remote_copy(
            total.at[part], sum_in.at[part], s_send.at[sem], s_recv.at[sem],
            device_id=across, device_id_type=MESH,
        )

    for copy in bra_copies:
        copy.wait()
    contract(app_own, 0, 8, 0, nbr * BLK, False)
    scatter(8, sb_own, rb_own, 4)

    boxes = ((sb0, rb0), (sb1, rb1), (sb2, rb2), (sb3, rb3))
    hop_own = hop(sum_own, 0, 8, 4)
    hops = [hop(sum_oth, e0, ne, c) for c, (e0, ne) in enumerate(CHUNKS)]

    def finish(c):
        e0, ne = CHUNKS[c]
        gather(ne, *boxes[c], c, sum_oth, e0)

        @pl.when(mine)
        def _():
            hops[c].start()

    for c, (e0, ne) in enumerate(CHUNKS):
        first = True
        todo = [(y_copies[i], r0, n) for i, (cc, r0, n) in enumerate(PIECES) if cc == c]
        if c < len(CHUNKS) - 1:
            for copy, _, _ in todo:
                copy.wait_recv()
            contract(app_oth, e0, ne, 0, nbr * BLK, False)
        else:
            for copy, r0, n in todo:
                copy.wait_recv()
                contract(app_oth, e0, ne, r0 * BLK, n * BLK, not first)
                first = False
        scatter(ne, *boxes[c], c)
        if c == 0:
            gather(8, sb_own, rb_own, 4, sum_own, 0)

            @pl.when(jnp.logical_not(mine))
            def _():
                hop_own.start()
        else:
            finish(c - 1)
    finish(len(CHUNKS) - 1)

    @pl.when(mine)
    def _():
        hop_own.wait_recv()
        sum_in[...] = sum_in[...] + sum_own[...]

    @pl.when(jnp.logical_not(mine))
    def _():
        for copy in hops:
            copy.wait_recv()
        sum_in[...] = sum_in[...] + sum_oth[...]

    for e in range(8):
        j = jl[8 * b + e]
        s = sl[8 * b + e]
        at = pl.ds(e * SEG, SEG)
        value = sum_in[at, :]
        allowed = (jnp.abs(j - ju[...]) <= 1) & (su[...] != s)
        stage[at, :] = jnp.where(allowed, value * value, jnp.zeros_like(value))
    for t in range(SEG):
        out[:, t * 128:t * 128 + 128] = stage[pl.ds(t, 8, stride=SEG), :]

    for copy in y_copies:
        copy.wait_send()

    @pl.when(b < last)
    def _():
        to_next.wait_send()

    @pl.when(b > 0)
    def _():
        to_prev.wait_send()

    @pl.when(mine)
    def _():
        for copy in hops:
            copy.wait_send()

    @pl.when(jnp.logical_not(mine))
    def _():
        hop_own.wait_send()


def on_device(bra, dipole, block_cols, ket, j_upper, sym_upper, j_lower, sym_lower):
    rows, upper = bra.shape
    half = ket.shape[1]
    nbr = rows // BLK
    vmem = pl.BlockSpec(memory_space=pltpu.VMEM)
    smem = pl.BlockSpec(memory_space=pltpu.SMEM)
    hbm = pl.BlockSpec(memory_space=pl.ANY)
    box = lambda ne: pltpu.VMEM((PLANE * ne * SEG, 128), BF16)
    boxes = [box(8)] * 2
    for _, ne in CHUNKS:
        boxes += [box(ne)] * 2
    dma = lambda n: pltpu.SemaphoreType.DMA((n,))
    flops = 2 * rows * 8 * BLK * half + 2 * rows * 2 * half * upper
    return pl.pallas_call(
        kernel,
        out_shape=jax.ShapeDtypeStruct((8, upper), F32),
        in_specs=[smem, smem, smem, vmem, vmem, hbm, hbm, hbm],
        out_specs=vmem,
        scratch_shapes=[
            pltpu.VMEM((upper // NT, rows, NT), BF16),
            pltpu.VMEM(dipole.shape, BF16),
            pltpu.VMEM((nbr, BLK, half), BF16),
            pltpu.VMEM((nbr + 2 * REACH, BLK, half), BF16),
            pltpu.VMEM((half, half), BF16),
            pltpu.VMEM((half, rows), BF16),
            pltpu.VMEM((half, rows), BF16),
            pltpu.VMEM((half * SEG, 128), F32),
            *boxes,
            pltpu.VMEM((8 * SEG, 128), F32),
            pltpu.VMEM((8 * SEG, 128), F32),
            pltpu.VMEM((8 * SEG, 128), F32),
            dma(upper // NT), dma(nbr // DIP_ROWS), dma(2), dma(2), dma(2),
            dma(len(PIECES)), dma(len(PIECES)), dma(5), dma(5), dma(5), dma(5),
        ],
        compiler_params=pltpu.CompilerParams(
            collective_id=0, has_side_effects=True, vmem_limit_bytes=56 * 1024 * 1024
        ),
        cost_estimate=pl.CostEstimate(flops=flops, bytes_accessed=28 * 1024 * 1024, transcendentals=0),
    )(
        block_cols, j_lower, sym_lower,
        j_upper.reshape(upper // 128, 128), sym_upper.reshape(upper // 128, 128),
        bra, dipole, ket.reshape(nbr, BLK, half),
    )


def solution(mesh):
    return jax.shard_map(
        on_device,
        mesh=mesh,
        in_specs=(
            P("basis", "grp"),
            P("basis", None, None, None),
            P("basis", None),
            P("basis", "grp"),
            P("grp"),
            P("grp"),
            P(),
            P(),
        ),
        out_specs=P("basis", "grp"),
        check_vma=False,
    )
```

time: 773 us -> 81.2 us (0.11)
  waiting for transfers between devices: 677 us -> 0 us
  Pallas kernels: 0 us -> 78.1 us
  matrix products: 40 us -> 0 us
  local copies, waits for them, and re-layouts: 24.5 us -> 2.84 us
  between operations: 13.5 us -> 0.01 us
  other arithmetic: 8.51 us -> 0 us
  starting transfers between devices: 7.84 us -> 0 us
    psum x1 -> x0, waiting for transfers between devices: 654 us -> none  [on_device(): total = lax.psum(partial_value, 'basis')]
    pallas_call x0 -> x1, Pallas kernels: none -> 78.1 us  [on_device(): pl.pallas_call(kernel, out_shape=jax.ShapeDtypeStruct((8, upper), F32), i...]
    dot_general x4 -> x0, matrix products: 40 us -> none  [the longest x2 22.2 us: apply_dipole(): jnp.einsum('rkij,rkjp->rip', dipole, picked, preferred_element_type=jnp.f...]
    ppermute x5 -> x0, waiting for transfers between devices: 22.7 us -> none  [the longest x1 20.6 us: from_behind(): return lax.ppermute(block, axis, route)]
    gather x2 -> x0, local copies, waits for them, and re-layouts: 19.5 us -> none  [apply_dipole(): picked = ext_blocks[local_cols]]
    ppermute x5 -> x0, starting transfers between devices: 7.84 us -> none  [the longest x2 4.99 us: with_halo(): lax.ppermute(tail, axis, [(i, (i + 1) % count) for i in range(ends)])]
  transfers between devices with their start and end apart: 6 -> 0, of which waited for: 3 -> 0; matrix products, arithmetic and copies ran while one was open for 5% -> 0% of each run, Pallas kernels for 0% -> 0%
where the time goes in v1:
time: 81.2 us; the launch traced here: 80.9 us
  Pallas kernels  78.1 us (96%)
  local copies, waits for them, and re-layouts  2.84 us (3%)
    pallas_call x1, Pallas kernels, on_device(): pl.pallas_call(kernel, out_shape=jax.ShapeDtypeStruct((8, upper), F32), i...  78.1 us
    unnamed x2, local copies, waits for them, and re-layouts  2.84 us

profile of v1, /device:TPU:8, one launch (start us, length us, event | category | flops | bytes accessed | tf_op | source)
XLA Modules:
  0.0 80.9 jit_solution(14153871529795471484)
XLA Ops:
  0.0 1.4 %copy.9.cols = s32[32,8]{1,0:T(8,128)} copy(s32[32,8]{0,1:T(8,128)} %param.10) | data formatting | bytes 2048 | tf_op args[2]
  1.4 78.1 %shard_map.82 = f32[8,2048]{1,0:T(8,128)} custom-call(s32[32,8]{1,0:T(8,128)} %copy.9.cols, s32[512]{0:T(512)} %jl.1, s32[512]{0:T(512)} %sl.1, s32[16,128]{1,0:T(8,128)} %bitcast.4, s32[16,128]{1,0:T(8,128)} %bitcast.5, bf16[4096,2048]{1,0:T(8,128)(2,1)} %bra_hbm.1, bf16[32,8,128,128]{3,2,1,0:T(8,128)(2,1)} %dip_hbm.1, bf16[32,128,256]{2,1,0:T(8,128)(2,1)} %bitcast.3), custom_call_target="tpu_custom_call" | custom-call | flops 10737418240 | bytes 29360128 | tf_op jit(solution)/shard_map/pallas_call | solution.py:320
  79.5 1.5 %copy.11 = f32[8,2048]{1,0:T(8,128)} copy(f32[8,2048]{1,0:T(8,128)} %shard_map.82) | data formatting | bytes 131072

commit v2 on v0

v2 whole, which is shorter than its diff:
```python
import jax
import jax.numpy as jnp
from jax import lax
from jax.experimental import pallas as pl
from jax.experimental.pallas import tpu as pltpu
from jax.sharding import PartitionSpec as P

MESH = pl.DeviceIdType.MESH
F32 = jnp.float32
BF16 = jnp.bfloat16

REACH = 8
BLK = 128
PLANE = 32
LINE = 8
SEG = 16
NT = 512

CHIPS = PLANE // 2
SHIFTS = sorted(
    ((dx, dz) for dz in range(4) for dx in range(4) if dx or dz),
    key=lambda t: -min(t[0], 4 - t[0]) - min(t[1], 4 - t[1]),
)
CHUNKS = ((0, 4), (4, 2), (6, 1), (7, 1))
LAST = len(CHUNKS) - 1
PIECES = (
    (0, 8, 4), (0, 12, 4), (0, 16, 4), (0, 20, 4), (1, 8, 16),
    (0, 0, 8), (0, 24, 8), (1, 0, 8), (1, 24, 8),
    (2, 8, 16), (2, 0, 8), (2, 24, 8),
    (3, 8, 16), (3, 0, 8), (3, 24, 4), (3, 28, 4),
)
DIP_ROWS = 4
ARRIVALS = (
    (0, 8, 16), (1, 8, 16), (0, 0, 8), (0, 24, 8), (1, 0, 8), (1, 24, 8),
    (2, 8, 16), (2, 0, 8), (2, 24, 8), (3, 8, 16), (3, 0, 8), (3, 24, 4), (3, 28, 4),
)
INNER = ((8, (0,)), (12, (1,)), (16, (2,)), (20, (3, 4)))
OUTER = ((0, ()), (4, (5,)), (24, ()), (28, (6, 7, 8, 9, 10, 11, 12, 13, 14, 15)))
STEPS = INNER + OUTER
RELAY = 10


def kernel(
    cols_hbm, jl_hbm, sl_hbm, ju_hbm, su_hbm, bra_hbm, dip_hbm, ket_hbm, out,
    cols, jl, sl, ju, su,
    bra, dip, ket_own, ket_ext, relay, perm, app_own, app_oth, mask,
    acc_own, acc0, acc1, acc2, acc3,
    stage_own, stage0, stage1, stage2, stage3, pair_own, pair0, pair1, pair2,
    sb_own, rb_own, sb0, rb0, sb1, rb1, sb2, rb2, sb3, rb3,
    sum_own, sum_oth, sum_in,
    small_sem, bra_sem, dip_sem, ket_sem, halo_send, halo_recv, corner_send, corner_recv,
    y_send, y_recv, pair_send, pair_recv, a_send, a_recv, s_send, s_recv, round_sem,
):
    b = lax.axis_index("basis")
    g = lax.axis_index("grp")
    yh = b // PLANE
    me = b % PLANE
    nbr = dip_hbm.shape[0]
    last = 2 * PLANE - 1
    low, high = PLANE - 1, PLANE
    mine = yh == g
    theirs = yh != g
    across = ((1 - yh) * PLANE + me, g)
    partner = (b, 1 - g)

    def tell(sem, device):
        pl.semaphore_signal(sem, inc=1, device_id=device, device_id_type=MESH)

    barrier = pltpu.get_barrier_semaphore()
    tell(barrier, partner)
    tell(barrier, across)
    for s in range(1, LINE):
        tell(barrier, (yh * PLANE + (me ^ s), g))
    for s in range(1, PLANE // LINE):
        tell(barrier, (yh * PLANE + (me ^ (s * LINE)), g))

    small = [
        pltpu.make_async_copy(src, dst, small_sem.at[i])
        for i, (src, dst) in enumerate(((cols_hbm, cols), (jl_hbm, jl), (sl_hbm, sl), (ju_hbm, ju), (su_hbm, su)))
    ]
    ket_copies = [
        pltpu.make_async_copy(ket_hbm, ket_own, ket_sem.at[0]),
        pltpu.make_async_copy(ket_hbm, ket_ext.at[pl.ds(REACH, nbr)], ket_sem.at[1]),
    ]
    dip_copies = {}
    for i, (r0, _) in enumerate(STEPS):
        rows = pl.ds(r0, DIP_ROWS)
        dip_copies[r0] = pltpu.make_async_copy(dip_hbm.at[rows], dip.at[rows], dip_sem.at[i])
    bra_copies = [
        pltpu.make_async_copy(bra_hbm.at[:, pl.ds(n * NT, NT)], bra.at[n], bra_sem.at[n])
        for n in range(bra.shape[0])
    ]
    small[0].start()
    ket_copies[0].start()
    for r0, _ in STEPS[:4]:
        dip_copies[r0].start()
    ket_copies[1].start()
    for r0, _ in STEPS[4:]:
        dip_copies[r0].start()
    @pl.when(me > 0)
    def _():
        tell(barrier, (b - 1, g))

    @pl.when(me < low)
    def _():
        tell(barrier, (b + 1, g))

    at_low, at_high = b == low, b == high
    relays_up = [high + RELAY * j for j in (1, 2, 3)]
    relays_down = [RELAY * j for j in (0, 1, 2)]
    is_up = (b == relays_up[0]) | (b == relays_up[1]) | (b == relays_up[2])
    is_down = (b == relays_down[0]) | (b == relays_down[1]) | (b == relays_down[2])

    @pl.when(at_low)
    def _():
        for peer in [high] + relays_up + relays_down:
            tell(barrier, (peer, g))

    @pl.when(at_high)
    def _():
        for peer in [low] + relays_up + relays_down:
            tell(barrier, (peer, g))

    @pl.when(is_up | is_down)
    def _():
        tell(barrier, (low, g))
        tell(barrier, (high, g))

    size = perm.shape[0]
    place = lax.broadcasted_iota(jnp.int32, (size, size), 0)
    state = lax.broadcasted_iota(jnp.int32, (size, size), 1)
    region = place & (PLANE - 1)
    wanted = (2 * (region & (CHIPS - 1)) + region // CHIPS) * 8 + place // PLANE
    perm[...] = jnp.where(state == wanted, 1.0, 0.0).astype(BF16)

    def apply_rows(r0, n, ket, base):
        def one(i, carry):
            r = r0 + i
            top = ket.shape[0] - 1
            blocks = [ket[jnp.clip(cols[k, r] - base, 0, top)] for k in range(cols.shape[0])]
            row = jnp.concatenate([dip[r, k] for k in range(cols.shape[0])], axis=1)
            value = jnp.dot(row, jnp.concatenate(blocks, axis=0), preferred_element_type=F32)
            turned = lax.dot_general(
                perm[...], value.astype(BF16), (((1,), (1,)), ((), ())), preferred_element_type=F32
            )
            app_own[:, pl.ds(pl.multiple_of(r * BLK, BLK), BLK)] = turned.astype(BF16)
            return carry

        lax.fori_loop(0, n, one, 0)

    def to_next(dst):
        return pltpu.make_async_remote_copy(
            ket_hbm.at[pl.ds(nbr - REACH, REACH)], ket_ext.at[pl.ds(0, REACH)],
            halo_send.at[0], halo_recv.at[0], device_id=(dst, g), device_id_type=MESH,
        )

    def to_prev(dst):
        return pltpu.make_async_remote_copy(
            ket_hbm.at[pl.ds(0, REACH)], ket_ext.at[pl.ds(REACH + nbr, REACH)],
            halo_send.at[1], halo_recv.at[1], device_id=(dst, g), device_id_type=MESH,
        )

    next_copy, prev_copy = to_next(jnp.minimum(b + 1, last)), to_prev(jnp.maximum(b - 1, 0))
    quarter = REACH // 4

    def corner(src, dst, sem, device):
        return pltpu.make_async_remote_copy(
            src, dst, corner_send.at[sem], corner_recv.at[sem], device_id=(device, g), device_id_type=MESH
        )

    def ket_part(start, j):
        return ket_hbm.at[pl.ds(start + quarter * j, quarter)]

    def ext_part(start, j):
        return ket_ext.at[pl.ds(start + quarter * j, quarter)]

    up_first = [corner(ket_part(nbr - REACH, 0), ext_part(0, 0), 0, high)]
    up_first += [corner(ket_part(nbr - REACH, j), relay, j, high + RELAY * j) for j in (1, 2, 3)]
    up_second = [corner(relay, ext_part(0, j), j, high) for j in (1, 2, 3)]
    down_first = [corner(ket_part(0, 3), ext_part(REACH + nbr, 3), 3, low)]
    down_first += [corner(ket_part(0, j), relay, j, RELAY * j) for j in (0, 1, 2)]
    down_second = [corner(relay, ext_part(REACH + nbr, j), j, low) for j in (0, 1, 2)]

    def relay_on():
        for j in (1, 2, 3):
            @pl.when(b == high + RELAY * j)
            def _():
                up_first[j].wait_recv()
                up_second[j - 1].start()
        for j in (0, 1, 2):
            @pl.when(b == RELAY * j)
            def _():
                down_first[j + 1].wait_recv()
                down_second[j].start()

    def halo_wait():
        ket_copies[1].wait()

        @pl.when((b > 0) & (b != high))
        def _():
            next_copy.wait_recv()

        @pl.when((b < last) & (b != low))
        def _():
            prev_copy.wait_recv()

        @pl.when(at_high)
        def _():
            up_first[0].wait_recv()
            for copy in up_second:
                copy.wait_recv()

        @pl.when(at_low)
        def _():
            down_first[0].wait_recv()
            for copy in down_second:
                copy.wait_recv()

    y_copies = []
    for i, (c, r0, n) in enumerate(PIECES):
        e0, ne = CHUNKS[c]
        part = (pl.ds(e0 * PLANE, ne * PLANE), pl.ds(r0 * BLK, n * BLK))
        y_copies.append(
            pltpu.make_async_remote_copy(
                app_own.at[part], app_oth.at[part], y_send.at[i], y_recv.at[i],
                device_id=partner, device_id_type=MESH,
            )
        )

    def enter():
        many = jnp.where(at_low | at_high, 7, jnp.where(is_up | is_down, 2, 0))
        ends = jnp.where(me > 0, 1, 0) + jnp.where(me < low, 1, 0)
        pl.semaphore_wait(barrier, LINE + PLANE // LINE + ends + many)

        @pl.when((b < last) & (b != low))
        def _():
            next_copy.start()

        @pl.when((b > 0) & (b != high))
        def _():
            prev_copy.start()

        @pl.when(at_low)
        def _():
            for copy in up_first:
                copy.start()

        @pl.when(at_high)
        def _():
            for copy in down_first:
                copy.start()

    def apply_step(r0, ready, ket, base):
        dip_copies[r0].wait()
        apply_rows(r0, DIP_ROWS, ket, base)
        if r0 == INNER[0][0]:
            enter()
        for k in ready:
            y_copies[k].start()

    def spread(value, stage, ne, first):
        for h in range(value.shape[1] // 128):
            for q in range(value.shape[0] // 8):
                e, o = q // (PLANE // 8), (q % (PLANE // 8)) * 8
                at = pl.ds(o * SEG * ne + e * SEG + first + h, 8, stride=SEG * ne)
                stage[at, :] = value[q * 8:q * 8 + 8, h * 128:h * 128 + 128]

    def contract(lhs, acc, stage, e0, ne, r0, n, begin, end):
        k = pl.ds(r0 * BLK, n * BLK)

        def one(t, carry):
            value = jnp.dot(
                lhs[pl.ds(e0 * PLANE, ne * PLANE), k], bra[t, k, :], preferred_element_type=F32
            )
            if not begin:
                value = value + acc[t]
            if end:
                spread(value, stage, ne, t * (NT // 128))
            else:
                acc[t] = value
            return carry

        if ne > 2:
            lax.fori_loop(0, bra.shape[0], one, 0)
        else:
            for t in range(bra.shape[0]):
                one(t, 0)

    core = me & 1
    chip = me // 2

    def meet(ne, stage, pair, sem):
        rows = CHIPS * ne * SEG
        theirs_at = pl.ds(pl.multiple_of((1 - core) * rows, rows), rows)
        return pltpu.make_async_remote_copy(
            stage.at[theirs_at], pair, pair_send.at[sem], pair_recv.at[sem],
            device_id=(b ^ 1, g), device_id_type=MESH,
        )

    def scatter(ne, stage, pair, sb, rb, sem):
        rows = ne * SEG
        meet(ne, stage, pair, sem).wait()

        def one(o, carry):
            at = pl.ds(pl.multiple_of(o * 4 * rows, 4 * rows), 4 * rows)
            own = pl.ds(pl.multiple_of(core * CHIPS * rows + o * 4 * rows, 4 * rows), 4 * rows)
            sb[at, :] = (stage[own, :] + pair[at, :]).astype(BF16)
            return carry

        lax.fori_loop(0, CHIPS // 4, one, 0)
        for slot, (dx, dz) in enumerate(SHIFTS):
            owner = (chip // 4 + dz) % 4 * 4 + (chip % 4 + dx) % 4
            pltpu.make_async_remote_copy(
                sb.at[pl.ds(pl.multiple_of(owner * rows, rows), rows)], rb.at[pl.ds(slot * rows, rows)],
                a_send.at[sem], a_recv.at[sem],
                device_id=(yh * PLANE + 2 * owner + core, g), device_id_type=MESH,
            ).start()

    def take(ne, sb, rb, sem, total, e0):
        rows = ne * SEG
        pltpu.make_async_remote_copy(
            sb.at[pl.ds(0, (CHIPS - 1) * rows)], rb, a_send.at[sem], a_recv.at[sem],
            device_id=partner, device_id_type=MESH,
        ).wait()
        add_up(ne, sb, chip, rb, CHIPS - 1, total, e0)

    def add_up(ne, sb, region, rb, slots, total, e0):
        rows = ne * SEG

        def one(s, value):
            return value + rb[pl.ds(pl.multiple_of(s * rows, rows), rows), :].astype(F32)

        value = sb[pl.ds(pl.multiple_of(region * rows, rows), rows), :].astype(F32)
        total[pl.ds(e0 * SEG, rows), :] = lax.fori_loop(0, slots, one, value)

    def scatter_last(ne, stage, sb, rb, plane, begin, slot, sem):
        rows = ne * SEG

        def send(s, carry):
            owner = lax.rem(me + s, PLANE)
            region = (owner & 1) * CHIPS + owner // 2
            pltpu.make_async_remote_copy(
                sb.at[pl.ds(pl.multiple_of(region * rows, rows), rows)],
                rb.at[pl.ds(pl.multiple_of((slot + s - begin) * rows, rows), rows)],
                a_send.at[sem], a_recv.at[sem],
                device_id=(plane * PLANE + owner, g), device_id_type=MESH,
            ).start()
            return carry

        lax.fori_loop(begin, PLANE, send, 0)

    def all_of(ne, sb, rb, begin, slot, sem):
        rows = ne * SEG
        return pltpu.make_async_remote_copy(
            sb.at[pl.ds(0, (PLANE - begin) * rows)], rb.at[pl.ds(slot * rows, (PLANE - begin) * rows)],
            a_send.at[sem], a_recv.at[sem], device_id=partner, device_id_type=MESH,
        )

    def hop(total, e0, ne, sem):
        part = pl.ds(e0 * SEG, ne * SEG)
        return pltpu.make_async_remote_copy(
            total.at[part], sum_in.at[part], s_send.at[sem], s_recv.at[sem],
            device_id=across, device_id_type=MESH,
        )

    OWN = LAST + 1
    hop_own = hop(sum_own, 0, 8, OWN)
    hops = [hop(sum_oth, e0, ne, c) for c, (e0, ne) in enumerate(CHUNKS[:LAST])]
    boxes = ((sb0, rb0), (sb1, rb1), (sb2, rb2))
    stages = (stage0, stage1, stage2, stage3)
    pairs = (pair0, pair1, pair2)

    def finish(c):
        e0, ne = CHUNKS[c]
        take(ne, *boxes[c], c, sum_oth, e0)

        @pl.when(mine)
        def _():
            hops[c].start()

    def main():
        small[0].wait()
        ket_copies[0].wait()
        for r0, ready in INNER:
            apply_step(r0, ready, ket_own, b * nbr)
            if r0 == INNER[1][0]:
                for s in range(1, PLANE // LINE):
                    tell(round_sem.at[0], (yh * PLANE + (me ^ (s * LINE)), g))
        for copy in bra_copies:
            copy.start()
        for copy in small[1:]:
            copy.start()
        relay_on()
        for copy in bra_copies:
            copy.wait()
        contract(app_own, acc_own, stage_own, 0, 8, REACH, nbr - 2 * REACH, True, False)
        pl.semaphore_wait(round_sem.at[0], PLANE // LINE - 1)
        tell(round_sem.at[1], across)
        halo_wait()
        for r0, ready in OUTER:
            apply_step(r0, ready, ket_ext, b * nbr - REACH)
        contract(app_own, acc_own, stage_own, 0, 8, 0, REACH, False, False)
        contract(app_own, acc_own, stage_own, 0, 8, nbr - REACH, REACH, False, True)
        meet(8, stage_own, pair_own, OWN).start()
        pl.semaphore_wait(round_sem.at[1], 1)

    main()

    def rules():
        for copy in small[1:]:
            copy.wait()
        for e in range(8):
            allowed = (jnp.abs(jl[8 * b + e] - ju[...]) <= 1) & (su[...] != sl[8 * b + e])
            mask[pl.ds(e * SEG, SEG), :] = jnp.where(allowed, 1.0, 0.0)

    def finish_own():
        take(8, sb_own, rb_own, OWN, sum_own, 0)

        @pl.when(theirs)
        def _():
            hop_own.start()

    accs = (acc0, acc1, acc2, acc3)
    seen = [0] * len(CHUNKS)
    for i, (c, r0, n) in enumerate(ARRIVALS):
        e0, ne = CHUNKS[c]
        for copy, (cc, p0, m) in zip(y_copies, PIECES):
            if cc == c and r0 <= p0 and p0 + m <= r0 + n:
                copy.wait_recv()
        full = seen[c] + n == nbr
        contract(app_oth, accs[c], stages[c], e0, ne, r0, n, seen[c] == 0, full)
        seen[c] += n
        if full and c < LAST:
            meet(ne, stages[c], pairs[c], c).start()
        if i == 0:
            scatter(8, stage_own, pair_own, sb_own, rb_own, OWN)
        if i == 3:
            finish_own()
        if i == 5:
            rules()
        if i == 8:
            finish(1)
        if full and c < LAST:
            scatter(ne, stages[c], pairs[c], *boxes[c], c)
        if i == 6:
            finish(0)
    e0, ne = CHUNKS[LAST]
    for q in range(4):
        at = pl.ds(q * PLANE // 4 * SEG, PLANE // 4 * SEG)
        sb3[at, :] = stage3[at, :].astype(BF16)

    @pl.when(mine)
    def _():
        scatter_last(ne, stage3, sb3, rb3, 1 - yh, 0, PLANE - 1, LAST)
        finish(LAST - 1)
        hop_own.wait_recv()
        sum_in[...] = sum_in[...] + sum_own[...]
        all_of(ne, sb3, rb3, 0, PLANE - 1, LAST).wait_send()

    @pl.when(theirs)
    def _():
        scatter_last(ne, stage3, sb3, rb3, yh, 1, 0, LAST + 2)
        finish(LAST - 1)
        kept = e0 * SEG
        for copy in hops:
            copy.wait_recv()
        sum_in[pl.ds(0, kept), :] = sum_in[pl.ds(0, kept), :] + sum_oth[pl.ds(0, kept), :]
        all_of(ne, sb3, rb3, 1, 0, LAST + 2).wait()
        all_of(ne, sb3, rb3, 0, PLANE - 1, LAST).wait_recv()
        add_up(ne, sb3, core * CHIPS + chip, rb3, 2 * PLANE - 1, sum_in, e0)

    value = sum_in[...]
    stage3[pl.ds(0, 8 * SEG), :] = jnp.where(mask[...] > 0.5, value * value, jnp.zeros_like(value))
    for t in range(SEG):
        out[:, t * 128:t * 128 + 128] = stage3[pl.ds(t, 8, stride=SEG), :]

    for copy in y_copies:
        copy.wait_send()

    @pl.when((b < last) & (b != low))
    def _():
        next_copy.wait_send()

    @pl.when((b > 0) & (b != high))
    def _():
        prev_copy.wait_send()

    @pl.when(at_low)
    def _():
        for copy in up_first:
            copy.wait_send()

    @pl.when(at_high)
    def _():
        for copy in down_first:
            copy.wait_send()

    for j in (1, 2, 3):
        @pl.when(b == high + RELAY * j)
        def _():
            up_second[j - 1].wait_send()
    for j in (0, 1, 2):
        @pl.when(b == RELAY * j)
        def _():
            down_second[j].wait_send()

    @pl.when(mine)
    def _():
        for copy in hops:
            copy.wait_send()

    @pl.when(theirs)
    def _():
        hop_own.wait_send()


def on_device(bra, dipole, block_cols, ket, j_upper, sym_upper, j_lower, sym_lower):
    rows, upper = bra.shape
    half = ket.shape[1]
    nbr = rows // BLK
    hbm = pl.BlockSpec(memory_space=pl.ANY)
    dma = lambda n: pltpu.SemaphoreType.DMA((n,))
    box = lambda slots, ne: pltpu.VMEM((slots * ne * SEG, 128), BF16)
    boxes = []
    for ne in (8,) + tuple(ne for _, ne in CHUNKS[:LAST]):
        boxes += [box(CHIPS, ne), box(CHIPS - 1, ne)]
    boxes += [box(PLANE, CHUNKS[LAST][1]), box(2 * PLANE - 1, CHUNKS[LAST][1])]
    sums = pltpu.VMEM((8 * SEG, 128), F32)
    accs = [pltpu.VMEM((upper // NT, ne * PLANE, NT), F32) for ne in (8,) + tuple(ne for _, ne in CHUNKS)]
    sizes = (8,) + tuple(ne for _, ne in CHUNKS)
    stages = [pltpu.VMEM((PLANE * ne * SEG, 128), F32) for ne in sizes]
    pairs = [pltpu.VMEM((CHIPS * ne * SEG, 128), F32) for ne in sizes[:-1]]
    whole = pltpu.SMEM(j_lower.shape, jnp.int32)
    segments = pltpu.VMEM((upper // 128, 128), jnp.int32)
    flops = 2 * rows * 8 * BLK * half + 2 * rows * 2 * half * upper
    return pl.pallas_call(
        kernel,
        out_shape=jax.ShapeDtypeStruct((8, upper), F32),
        in_specs=[hbm] * 8,
        out_specs=pl.BlockSpec(memory_space=pltpu.VMEM),
        scratch_shapes=[
            pltpu.SMEM(block_cols.shape[::-1], jnp.int32), whole, whole, segments, segments,
            pltpu.VMEM((upper // NT, rows, NT), BF16),
            pltpu.VMEM(dipole.shape, BF16),
            pltpu.VMEM((nbr, BLK, half), BF16),
            pltpu.VMEM((nbr + 2 * REACH, BLK, half), BF16),
            pltpu.VMEM((REACH // 4, BLK, half), BF16),
            pltpu.VMEM((half, half), BF16),
            pltpu.VMEM((half, rows), BF16),
            pltpu.VMEM((half, rows), BF16),
            sums,
            *accs,
            *stages,
            *pairs,
            *boxes,
            sums, sums, sums,
            dma(5), dma(upper // NT), dma(len(STEPS)), dma(2), dma(2), dma(2), dma(4), dma(4),
            dma(len(PIECES)), dma(len(PIECES)), dma(LAST + 2), dma(LAST + 2), dma(LAST + 3), dma(LAST + 3), dma(LAST + 2), dma(LAST + 2),
            pltpu.SemaphoreType.REGULAR((2,)),
        ],
        compiler_params=pltpu.CompilerParams(
            collective_id=0, has_side_effects=True, vmem_limit_bytes=56 * 1024 * 1024
        ),
        cost_estimate=pl.CostEstimate(flops=flops, bytes_accessed=28 * 1024 * 1024, transcendentals=0),
    )(
        block_cols.T, j_lower, sym_lower,
        j_upper.reshape(upper // 128, 128), sym_upper.reshape(upper // 128, 128),
        bra, dipole, ket.reshape(nbr, BLK, half),
    )


def solution(mesh):
    return jax.shard_map(
        on_device,
        mesh=mesh,
        in_specs=(
            P("basis", "grp"),
            P("basis", None, None, None),
            P("basis", None),
            P("basis", "grp"),
            P("grp"),
            P("grp"),
            P(),
            P(),
        ),
        out_specs=P("basis", "grp"),
        check_vma=False,
    )
```

time: 773 us -> 68.8 us (0.09)
  waiting for transfers between devices: 677 us -> 0 us
  Pallas kernels: 0 us -> 66.9 us
  matrix products: 40 us -> 0 us
  local copies, waits for them, and re-layouts: 24.5 us -> 1.47 us
  between operations: 13.5 us -> 0.01 us
  other arithmetic: 8.51 us -> 0 us
  starting transfers between devices: 7.84 us -> 0 us
    psum x1 -> x0, waiting for transfers between devices: 654 us -> none  [on_device(): total = lax.psum(partial_value, 'basis')]
    pallas_call x0 -> x1, Pallas kernels: none -> 66.9 us  [on_device(): pl.pallas_call(kernel, out_shape=jax.ShapeDtypeStruct((8, upper), F32), i...]
    dot_general x4 -> x0, matrix products: 40 us -> none  [the longest x2 22.2 us: apply_dipole(): jnp.einsum('rkij,rkjp->rip', dipole, picked, preferred_element_type=jnp.f...]
    ppermute x5 -> x0, waiting for transfers between devices: 22.7 us -> none  [the longest x1 20.6 us: from_behind(): return lax.ppermute(block, axis, route)]
    gather x2 -> x0, local copies, waits for them, and re-layouts: 19.5 us -> none  [apply_dipole(): picked = ext_blocks[local_cols]]
    ppermute x5 -> x0, starting transfers between devices: 7.84 us -> none  [the longest x2 4.99 us: with_halo(): lax.ppermute(tail, axis, [(i, (i + 1) % count) for i in range(ends)])]
  transfers between devices with their start and end apart: 6 -> 0, of which waited for: 3 -> 0; matrix products, arithmetic and copies ran while one was open for 5% -> 0% of each run, Pallas kernels for 0% -> 0%
where the time goes in v2:
time: 68.8 us; the launch traced here: 68.3 us
  Pallas kernels  66.9 us (97%)
  local copies, waits for them, and re-layouts  1.47 us (2%)
    pallas_call x1, Pallas kernels, on_device(): pl.pallas_call(kernel, out_shape=jax.ShapeDtypeStruct((8, upper), F32), i...  66.9 us
    unnamed x1, local copies, waits for them, and re-layouts  1.47 us

profile of v2, /device:TPU:8, one launch (start us, length us, event | category | flops | bytes accessed | tf_op | source)
XLA Modules:
  0.0 68.3 jit_solution(553384823512518822)
XLA Ops:
  0.0 66.9 %shard_map.82 = f32[8,2048]{1,0:T(8,128)} custom-call(s32[8,32]{1,0:T(8,128)} %bitcast.7, s32[512]{0:T(512)} %jl_hbm.1, s32[512]{0:T(512)} %sl_hbm.1, s32[16,128]{1,0:T(8,128)} %bitcast.5, s32[16,128]{1,0:T(8,128)} %bitcast.6, bf16[4096,2048]{1,0:T(8,128)(2,1)} %bra_hbm.1, bf16[32,8,128,128]{3,2,1,0:T(8,128)(2,1)} %dip_hbm.1, bf16[32,128,256]{2,1,0:T(8,128)(2,1)} %bitcast.4), custom_call_target="tpu_custom_call" | custom-call | flops 10737418240 | bytes 29360128 | tf_op jit(solution)/shard_map/pallas_call | solution.py:536
  66.9 1.5 %copy.10 = f32[8,2048]{1,0:T(8,128)} copy(f32[8,2048]{1,0:T(8,128)} %shard_map.82) | data formatting | bytes 131072

commit v3 on v2

--- a/solution.py
+++ b/solution.py
@@ -21,21 +21,21 @@
     ((dx, dz) for dz in range(4) for dx in range(4) if dx or dz),
     key=lambda t: -min(t[0], 4 - t[0]) - min(t[1], 4 - t[1]),
 )
+PLACES = [(dx, dz, dc) for dx, dz in SHIFTS + [(0, 0)] for dc in (1, 0)]
 CHUNKS = ((0, 4), (4, 2), (6, 1), (7, 1))
 LAST = len(CHUNKS) - 1
 PIECES = (
-    (0, 8, 4), (0, 12, 4), (0, 16, 4), (0, 20, 4), (1, 8, 16),
+    (0, 8, 2), (0, 10, 6), (0, 16, 4), (0, 20, 4), (1, 8, 16),
     (0, 0, 8), (0, 24, 8), (1, 0, 8), (1, 24, 8),
     (2, 8, 16), (2, 0, 8), (2, 24, 8),
-    (3, 8, 16), (3, 0, 8), (3, 24, 4), (3, 28, 4),
+    (3, 8, 16), (3, 0, 8), (3, 24, 6), (3, 30, 2),
 )
-DIP_ROWS = 4
 ARRIVALS = (
     (0, 8, 16), (1, 8, 16), (0, 0, 8), (0, 24, 8), (1, 0, 8), (1, 24, 8),
-    (2, 8, 16), (2, 0, 8), (2, 24, 8), (3, 8, 16), (3, 0, 8), (3, 24, 4), (3, 28, 4),
+    (2, 8, 16), (2, 0, 8), (2, 24, 8), (3, 8, 16), (3, 0, 8), (3, 24, 6), (3, 30, 2),
 )
-INNER = ((8, (0,)), (12, (1,)), (16, (2,)), (20, (3, 4)))
-OUTER = ((0, ()), (4, (5,)), (24, ()), (28, (6, 7, 8, 9, 10, 11, 12, 13, 14, 15)))
+INNER = ((8, 2, (0,)), (10, 6, (1,)), (16, 4, (2,)), (20, 4, (3, 4)))
+OUTER = ((0, 4, ()), (4, 4, (5,)), (24, 4, ()), (28, 4, (6, 7, 8, 9, 10, 11, 12, 13, 14, 15)))
 STEPS = INNER + OUTER
 RELAY = 10
 
@@ -83,19 +83,20 @@
         pltpu.make_async_copy(ket_hbm, ket_ext.at[pl.ds(REACH, nbr)], ket_sem.at[1]),
     ]
     dip_copies = {}
-    for i, (r0, _) in enumerate(STEPS):
-        rows = pl.ds(r0, DIP_ROWS)
+    for i, (r0, n, _) in enumerate(STEPS):
+        rows = pl.ds(r0, n)
         dip_copies[r0] = pltpu.make_async_copy(dip_hbm.at[rows], dip.at[rows], dip_sem.at[i])
     bra_copies = [
         pltpu.make_async_copy(bra_hbm.at[:, pl.ds(n * NT, NT)], bra.at[n], bra_sem.at[n])
         for n in range(bra.shape[0])
     ]
     small[0].start()
+    dip_copies[STEPS[0][0]].start()
     ket_copies[0].start()
-    for r0, _ in STEPS[:4]:
+    for r0, _, _ in STEPS[1:4]:
         dip_copies[r0].start()
     ket_copies[1].start()
-    for r0, _ in STEPS[4:]:
+    for r0, _, _ in STEPS[4:]:
         dip_copies[r0].start()
     @pl.when(me > 0)
     def _():
@@ -250,9 +251,9 @@
             for copy in down_first:
                 copy.start()
 
-    def apply_step(r0, ready, ket, base):
+    def apply_step(r0, n, ready, ket, base):
         dip_copies[r0].wait()
-        apply_rows(r0, DIP_ROWS, ket, base)
+        apply_rows(r0, n, ket, base)
         if r0 == INNER[0][0]:
             enter()
         for k in ready:
@@ -333,21 +334,17 @@
         value = sb[pl.ds(pl.multiple_of(region * rows, rows), rows), :].astype(F32)
         total[pl.ds(e0 * SEG, rows), :] = lax.fori_loop(0, slots, one, value)
 
-    def scatter_last(ne, stage, sb, rb, plane, begin, slot, sem):
+    def scatter_last(ne, sb, rb, plane, count, slot, sem):
         rows = ne * SEG
-
-        def send(s, carry):
-            owner = lax.rem(me + s, PLANE)
-            region = (owner & 1) * CHIPS + owner // 2
+        for s, (dx, dz, dc) in enumerate(PLACES[:count]):
+            to_chip = (chip // 4 + dz) % 4 * 4 + (chip % 4 + dx) % 4
+            to_core = core ^ dc
+            region = to_core * CHIPS + to_chip
             pltpu.make_async_remote_copy(
-                sb.at[pl.ds(pl.multiple_of(region * rows, rows), rows)],
-                rb.at[pl.ds(pl.multiple_of((slot + s - begin) * rows, rows), rows)],
+                sb.at[pl.ds(pl.multiple_of(region * rows, rows), rows)], rb.at[pl.ds((slot + s) * rows, rows)],
                 a_send.at[sem], a_recv.at[sem],
-                device_id=(plane * PLANE + owner, g), device_id_type=MESH,
+                device_id=(plane * PLANE + 2 * to_chip + to_core, g), device_id_type=MESH,
             ).start()
-            return carry
-
-        lax.fori_loop(begin, PLANE, send, 0)
 
     def all_of(ne, sb, rb, begin, slot, sem):
         rows = ne * SEG
@@ -381,15 +378,16 @@
     def main():
         small[0].wait()
         ket_copies[0].wait()
-        for r0, ready in INNER:
-            apply_step(r0, ready, ket_own, b * nbr)
+        for r0, n, ready in INNER:
+            apply_step(r0, n, ready, ket_own, b * nbr)
+            if r0 == INNER[0][0]:
+                for copy in bra_copies:
+                    copy.start()
+                for copy in small[1:]:
+                    copy.start()
             if r0 == INNER[1][0]:
                 for s in range(1, PLANE // LINE):
                     tell(round_sem.at[0], (yh * PLANE + (me ^ (s * LINE)), g))
-        for copy in bra_copies:
-            copy.start()
-        for copy in small[1:]:
-            copy.start()
         relay_on()
         for copy in bra_copies:
             copy.wait()
@@ -397,8 +395,8 @@
         pl.semaphore_wait(round_sem.at[0], PLANE // LINE - 1)
         tell(round_sem.at[1], across)
         halo_wait()
-        for r0, ready in OUTER:
-            apply_step(r0, ready, ket_ext, b * nbr - REACH)
+        for r0, n, ready in OUTER:
+            apply_step(r0, n, ready, ket_ext, b * nbr - REACH)
         contract(app_own, acc_own, stage_own, 0, 8, 0, REACH, False, False)
         contract(app_own, acc_own, stage_own, 0, 8, nbr - REACH, REACH, False, True)
         meet(8, stage_own, pair_own, OWN).start()
@@ -438,8 +436,6 @@
             finish_own()
         if i == 5:
             rules()
-        if i == 8:
-            finish(1)
         if full and c < LAST:
             scatter(ne, stages[c], pairs[c], *boxes[c], c)
         if i == 6:
@@ -451,7 +447,8 @@
 
     @pl.when(mine)
     def _():
-        scatter_last(ne, stage3, sb3, rb3, 1 - yh, 0, PLANE - 1, LAST)
+        scatter_last(ne, sb3, rb3, 1 - yh, PLANE, PLANE - 1, LAST)
+        finish(LAST - 2)
         finish(LAST - 1)
         hop_own.wait_recv()
         sum_in[...] = sum_in[...] + sum_own[...]
@@ -459,15 +456,23 @@
 
     @pl.when(theirs)
     def _():
-        scatter_last(ne, stage3, sb3, rb3, yh, 1, 0, LAST + 2)
+        scatter_last(ne, sb3, rb3, yh, PLANE - 1, 0, LAST + 2)
+        finish(LAST - 2)
         finish(LAST - 1)
         kept = e0 * SEG
         for copy in hops:
             copy.wait_recv()
         sum_in[pl.ds(0, kept), :] = sum_in[pl.ds(0, kept), :] + sum_oth[pl.ds(0, kept), :]
+        rows = ne * SEG
+        region = core * CHIPS + chip
+        value = sb3[pl.ds(pl.multiple_of(region * rows, rows), rows), :].astype(F32)
         all_of(ne, sb3, rb3, 1, 0, LAST + 2).wait()
+        for s in range(PLANE - 1):
+            value = value + rb3[pl.ds(s * rows, rows), :].astype(F32)
         all_of(ne, sb3, rb3, 0, PLANE - 1, LAST).wait_recv()
-        add_up(ne, sb3, core * CHIPS + chip, rb3, 2 * PLANE - 1, sum_in, e0)
+        for s in range(PLANE - 1, 2 * PLANE - 1):
+            value = value + rb3[pl.ds(s * rows, rows), :].astype(F32)
+        sum_in[pl.ds(e0 * SEG, rows), :] = value
 
     value = sum_in[...]
     stage3[pl.ds(0, 8 * SEG), :] = jnp.where(mask[...] > 0.5, value * value, jnp.zeros_like(value))

time: 68.8 us -> 66.7 us (0.969)
  Pallas kernels: 66.9 us -> 65.1 us
    pallas_call x1, Pallas kernels: 66.9 us -> 65.1 us  [on_device(): pl.pallas_call(kernel, out_shape=jax.ShapeDtypeStruct((8, upper), F32), i...]
where the time goes in v3:
time: 66.7 us; the launch traced here: 66.6 us
  Pallas kernels  65.1 us (98%)
  local copies, waits for them, and re-layouts  1.47 us (2%)
    pallas_call x1, Pallas kernels, on_device(): pl.pallas_call(kernel, out_shape=jax.ShapeDtypeStruct((8, upper), F32), i...  65.1 us
    unnamed x1, local copies, waits for them, and re-layouts  1.47 us

profile of v3, /device:TPU:8, one launch (start us, length us, event | category | flops | bytes accessed | tf_op | source)
XLA Modules:
  0.0 66.6 jit_solution(11602099278966326517)
XLA Ops:
  0.0 65.1 %shard_map.82 = f32[8,2048]{1,0:T(8,128)} custom-call(s32[8,32]{1,0:T(8,128)} %bitcast.7, s32[512]{0:T(512)} %jl_hbm.1, s32[512]{0:T(512)} %sl_hbm.1, s32[16,128]{1,0:T(8,128)} %bitcast.5, s32[16,128]{1,0:T(8,128)} %bitcast.6, bf16[4096,2048]{1,0:T(8,128)(2,1)} %bra_hbm.1, bf16[32,8,128,128]{3,2,1,0:T(8,128)(2,1)} %dip_hbm.1, bf16[32,128,256]{2,1,0:T(8,128)(2,1)} %bitcast.4), custom_call_target="tpu_custom_call" | custom-call | flops 10737418240 | bytes 29360128 | tf_op jit(solution)/shard_map/pallas_call | solution.py:541
  65.1 1.5 %copy.10 = f32[8,2048]{1,0:T(8,128)} copy(f32[8,2048]{1,0:T(8,128)} %shard_map.82) | data formatting | bytes 131072

commit v4 on v3

--- a/solution.py
+++ b/solution.py
@@ -25,7 +25,7 @@
 CHUNKS = ((0, 4), (4, 2), (6, 1), (7, 1))
 LAST = len(CHUNKS) - 1
 PIECES = (
-    (0, 8, 2), (0, 10, 6), (0, 16, 4), (0, 20, 4), (1, 8, 16),
+    (0, 8, 1), (0, 9, 3), (0, 12, 4), (0, 16, 4), (0, 20, 4), (1, 8, 16),
     (0, 0, 8), (0, 24, 8), (1, 0, 8), (1, 24, 8),
     (2, 8, 16), (2, 0, 8), (2, 24, 8),
     (3, 8, 16), (3, 0, 8), (3, 24, 6), (3, 30, 2),
@@ -34,10 +34,10 @@
     (0, 8, 16), (1, 8, 16), (0, 0, 8), (0, 24, 8), (1, 0, 8), (1, 24, 8),
     (2, 8, 16), (2, 0, 8), (2, 24, 8), (3, 8, 16), (3, 0, 8), (3, 24, 6), (3, 30, 2),
 )
-INNER = ((8, 2, (0,)), (10, 6, (1,)), (16, 4, (2,)), (20, 4, (3, 4)))
-OUTER = ((0, 4, ()), (4, 4, (5,)), (24, 4, ()), (28, 4, (6, 7, 8, 9, 10, 11, 12, 13, 14, 15)))
+INNER = ((8, 1, (0,)), (9, 3, (1,)), (12, 4, (2,)), (16, 4, (3,)), (20, 4, (4, 5)))
+OUTER = ((0, 4, ()), (4, 4, (6,)), (24, 4, ()), (28, 4, (7, 8, 9, 10, 11, 12, 13, 14, 15, 16)))
 STEPS = INNER + OUTER
-RELAY = 10
+UP = 24
 
 
 def kernel(
@@ -107,8 +107,8 @@
         tell(barrier, (b + 1, g))
 
     at_low, at_high = b == low, b == high
-    relays_up = [high + RELAY * j for j in (1, 2, 3)]
-    relays_down = [RELAY * j for j in (0, 1, 2)]
+    relays_up = [high + UP + 2 * j for j in (1, 2, 3)]
+    relays_down = [2 * j for j in (0, 1, 2)]
     is_up = (b == relays_up[0]) | (b == relays_up[1]) | (b == relays_up[2])
     is_down = (b == relays_down[0]) | (b == relays_down[1]) | (b == relays_down[2])
 
@@ -176,20 +176,20 @@
         return ket_ext.at[pl.ds(start + quarter * j, quarter)]
 
     up_first = [corner(ket_part(nbr - REACH, 0), ext_part(0, 0), 0, high)]
-    up_first += [corner(ket_part(nbr - REACH, j), relay, j, high + RELAY * j) for j in (1, 2, 3)]
+    up_first += [corner(ket_part(nbr - REACH, j), relay, j, high + UP + 2 * j) for j in (1, 2, 3)]
     up_second = [corner(relay, ext_part(0, j), j, high) for j in (1, 2, 3)]
     down_first = [corner(ket_part(0, 3), ext_part(REACH + nbr, 3), 3, low)]
-    down_first += [corner(ket_part(0, j), relay, j, RELAY * j) for j in (0, 1, 2)]
+    down_first += [corner(ket_part(0, j), relay, j, 2 * j) for j in (0, 1, 2)]
     down_second = [corner(relay, ext_part(REACH + nbr, j), j, low) for j in (0, 1, 2)]
 
     def relay_on():
         for j in (1, 2, 3):
-            @pl.when(b == high + RELAY * j)
+            @pl.when(b == high + UP + 2 * j)
             def _():
                 up_first[j].wait_recv()
                 up_second[j - 1].start()
         for j in (0, 1, 2):
-            @pl.when(b == RELAY * j)
+            @pl.when(b == 2 * j)
             def _():
                 down_first[j + 1].wait_recv()
                 down_second[j].start()
@@ -501,11 +501,11 @@
             copy.wait_send()
 
     for j in (1, 2, 3):
-        @pl.when(b == high + RELAY * j)
+        @pl.when(b == high + UP + 2 * j)
         def _():
             up_second[j - 1].wait_send()
     for j in (0, 1, 2):
-        @pl.when(b == RELAY * j)
+        @pl.when(b == 2 * j)
         def _():
             down_second[j].wait_send()
 

time: 66.7 us -> 66 us (0.990)
  Pallas kernels: 65.1 us -> 64.4 us
    pallas_call x1, Pallas kernels: 65.1 us -> 64.4 us  [on_device(): pl.pallas_call(kernel, out_shape=jax.ShapeDtypeStruct((8, upper), F32), i...]
where the time goes in v4:
time: 66 us; the launch traced here: 65.9 us
  Pallas kernels  64.4 us (98%)
  local copies, waits for them, and re-layouts  1.47 us (2%)
    pallas_call x1, Pallas kernels, on_device(): pl.pallas_call(kernel, out_shape=jax.ShapeDtypeStruct((8, upper), F32), i...  64.4 us
    unnamed x1, local copies, waits for them, and re-layouts  1.47 us

profile of v4, /device:TPU:8, one launch (start us, length us, event | category | flops | bytes accessed | tf_op | source)
XLA Modules:
  0.0 65.9 jit_solution(10042837988853502060)
XLA Ops:
  0.0 64.4 %shard_map.82 = f32[8,2048]{1,0:T(8,128)} custom-call(s32[8,32]{1,0:T(8,128)} %bitcast.7, s32[512]{0:T(512)} %jl_hbm.1, s32[512]{0:T(512)} %sl_hbm.1, s32[16,128]{1,0:T(8,128)} %bitcast.5, s32[16,128]{1,0:T(8,128)} %bitcast.6, bf16[4096,2048]{1,0:T(8,128)(2,1)} %bra_hbm.1, bf16[32,8,128,128]{3,2,1,0:T(8,128)(2,1)} %dip_hbm.1, bf16[32,128,256]{2,1,0:T(8,128)(2,1)} %bitcast.4), custom_call_target="tpu_custom_call" | custom-call | flops 10737418240 | bytes 29360128 | tf_op jit(solution)/shard_map/pallas_call | solution.py:541
  64.4 1.5 %copy.10 = f32[8,2048]{1,0:T(8,128)} copy(f32[8,2048]{1,0:T(8,128)} %shard_map.82) | data formatting | bytes 131072

commit v5 on v4

--- a/solution.py
+++ b/solution.py
@@ -66,14 +66,6 @@
     def tell(sem, device):
         pl.semaphore_signal(sem, inc=1, device_id=device, device_id_type=MESH)
 
-    barrier = pltpu.get_barrier_semaphore()
-    tell(barrier, partner)
-    tell(barrier, across)
-    for s in range(1, LINE):
-        tell(barrier, (yh * PLANE + (me ^ s), g))
-    for s in range(1, PLANE // LINE):
-        tell(barrier, (yh * PLANE + (me ^ (s * LINE)), g))
-
     small = [
         pltpu.make_async_copy(src, dst, small_sem.at[i])
         for i, (src, dst) in enumerate(((cols_hbm, cols), (jl_hbm, jl), (sl_hbm, sl), (ju_hbm, ju), (su_hbm, su)))
@@ -93,6 +85,15 @@
     small[0].start()
     dip_copies[STEPS[0][0]].start()
     ket_copies[0].start()
+
+    barrier = pltpu.get_barrier_semaphore()
+    tell(barrier, partner)
+    tell(barrier, across)
+    for s in range(1, LINE):
+        tell(barrier, (yh * PLANE + (me ^ s), g))
+    for s in range(1, PLANE // LINE):
+        tell(barrier, (yh * PLANE + (me ^ (s * LINE)), g))
+
     for r0, _, _ in STEPS[1:4]:
         dip_copies[r0].start()
     ket_copies[1].start()

time: 66 us -> 65.8 us (level)
  no operation moved by 1% of the time
where the time goes in v5:
time: 65.8 us; the launch traced here: 65.6 us
  Pallas kernels  64.1 us (97%)
  local copies, waits for them, and re-layouts  1.47 us (2%)
    pallas_call x1, Pallas kernels, on_device(): pl.pallas_call(kernel, out_shape=jax.ShapeDtypeStruct((8, upper), F32), i...  64.1 us
    unnamed x1, local copies, waits for them, and re-layouts  1.47 us

profile of v5, /device:TPU:8, one launch (start us, length us, event | category | flops | bytes accessed | tf_op | source)
XLA Modules:
  0.0 65.6 jit_solution(5558807066931240113)
XLA Ops:
  0.0 64.1 %shard_map.82 = f32[8,2048]{1,0:T(8,128)} custom-call(s32[8,32]{1,0:T(8,128)} %bitcast.7, s32[512]{0:T(512)} %jl_hbm.1, s32[512]{0:T(512)} %sl_hbm.1, s32[16,128]{1,0:T(8,128)} %bitcast.5, s32[16,128]{1,0:T(8,128)} %bitcast.6, bf16[4096,2048]{1,0:T(8,128)(2,1)} %bra_hbm.1, bf16[32,8,128,128]{3,2,1,0:T(8,128)(2,1)} %dip_hbm.1, bf16[32,128,256]{2,1,0:T(8,128)(2,1)} %bitcast.4), custom_call_target="tpu_custom_call" | custom-call | flops 10737418240 | bytes 29360128 | tf_op jit(solution)/shard_map/pallas_call | solution.py:542
  64.1 1.5 %copy.10 = f32[8,2048]{1,0:T(8,128)} copy(f32[8,2048]{1,0:T(8,128)} %shard_map.82) | data formatting | bytes 131072
